TPU v7x, 32 devices: a whole 2x2x4 slice. The times are simulated.
32 devices in a mesh: row: 4 (over y, core), col: 8 (over z, x).
Axes of the slice: x: 2, y: 2, z: 4, core: 2. Of those that a mesh axis runs over, the one named last changes fastest.
Arguments:
- amplitudes: bfloat16 [2048, 2048], P('row', 'col'), may hold values from -6 to 6
- integrals: bfloat16 [400, 400], replicated, may hold values from -0.3125 to 0.3125
- targets: int32 [110, 2048], replicated, may hold values from 0 to 2047
- pairs: int32 [110, 2048], replicated, may hold values from 0 to 399, as said below
- parity: int32 [110, 2048], replicated, may hold values 0 or 1
- alpha_window: int32 [768], P('row'), may hold values from 0 to 2047
- beta_window: int32 [768], P('col'), may hold values from 0 to 2047
Outputs:
- sigma: float32 [2048, 2048], P('row', 'col')
Inputs may be any that keep to these rules, and one draw needn't show every extreme that they name: Each string has 110 distinct pairs: for each of its 10 occupied orbitals l, the pairs k * 20 + l with k unoccupied or k = l.
All inputs are finite; a program needn't handle non-finite values.
Results may differ from a plain program's by a relative error of at most 0.0029.
Values may be sent and summed in bfloat16 or wider, within the bound.
A program may use at most 128 MiB of HBM per device.

v0:
```python
import jax
import jax.numpy as jnp
from jax import lax
from jax.sharding import PartitionSpec as P

ORB = 20


def window_lists(targets, pairs, parity, window):
    target_ids = jnp.take(targets, window, axis=1).T
    pair_ids = jnp.take(pairs, window, axis=1).T
    sign_values = 1.0 - 2.0 * jnp.take(parity, window, axis=1).T.astype(jnp.float32)
    return (target_ids, pair_ids, sign_values)


def transform_block(rows, pair_ids, swap_ids, sign_values, integrals):
    weighted = jnp.take(integrals, pair_ids, axis=0) * sign_values[..., None].astype(jnp.bfloat16)
    transformed = jnp.einsum(
        "wen,wel->wnl", weighted, rows, preferred_element_type=jnp.float32
    ).astype(jnp.bfloat16)
    columns = lax.broadcasted_iota(jnp.int32, (1, 1, ORB * ORB), 2)
    selector = jnp.where(swap_ids[..., None] == columns, sign_values[..., None], 0.0).astype(
        jnp.bfloat16
    )
    return jnp.einsum("wen,wnl->wel", selector, transformed, preferred_element_type=jnp.float32)


def window_terms(gathered, target_ids, pair_ids, sign_values, integrals):
    blocks = target_ids.shape[0] // 16
    width = gathered.shape[1]
    swap_ids = pair_ids % ORB * ORB + pair_ids // ORB

    def shaped(array):
        return array.reshape((blocks, 16) + array.shape[1:])

    def one_block(partial_value, inputs):
        block_targets, block_pairs, block_swaps, block_signs = inputs
        rows = jnp.take(gathered, block_targets, axis=0)
        picked = transform_block(rows, block_pairs, block_swaps, block_signs, integrals)
        partial_value = partial_value.at[block_targets.reshape(-1)].add(
            picked.reshape(-1, width), mode="drop"
        )
        return (partial_value, None)

    start = jnp.zeros((gathered.shape[0], width), jnp.float32)
    partial_value, unused = lax.scan(
        one_block,
        start,
        (shaped(target_ids), shaped(pair_ids), shaped(swap_ids), shaped(sign_values)),
    )
    return partial_value


def on_device(amplitudes, integrals, targets, pairs, parity, alpha_window, beta_window):
    alpha_targets, alpha_pairs, alpha_signs = window_lists(targets, pairs, parity, alpha_window)
    beta_targets, beta_pairs, beta_signs = window_lists(targets, pairs, parity, beta_window)
    mirrored = amplitudes.T
    alpha_columns = lax.all_gather(amplitudes, "row", axis=0, tiled=True)
    beta_columns = lax.all_gather(mirrored, "col", axis=0, tiled=True)
    alpha_terms = window_terms(alpha_columns, alpha_targets, alpha_pairs, alpha_signs, integrals)
    beta_terms = window_terms(beta_columns, beta_targets, beta_pairs, beta_signs, integrals)
    alpha_part = lax.psum_scatter(alpha_terms, "row", scatter_dimension=0, tiled=True)
    beta_part = lax.psum_scatter(beta_terms, "col", scatter_dimension=0, tiled=True)
    return alpha_part + beta_part.T


def solution(mesh):
    in_specs = (P("row", "col"), P(), P(), P(), P(), P("row"), P("col"))
    out_specs = P("row", "col")
    return jax.shard_map(
        on_device, mesh=mesh, in_specs=in_specs, out_specs=out_specs, check_vma=False
    )
```

profile of v0, /device:TPU:15, one launch (start us, length us, event | category | flops | bytes accessed | tf_op | source)
XLA Modules:
  0.0 1198.8 jit_solution(849876633468000202)
XLA Ops:
  27.5 720.7 %while.20 = (s32[]{:T(128)}, f32[2048,256]{1,0:T(8,128)S(1)}, s32[12,16,110]{2,1,0:T(8,128)}, s32[12,16,110]{2,1,0:T(8,128)}, bf16[12,16,110]{2,1,0:T(8,128)(2,1...) while((s32[]{:T(128)}, f32[2048,256]{1,0:T(8,128)S(1)}, ...), condition=%wide.region_2.5_spmd, body=%wide.region_0.4_spmd.sunk | while | flops 726287296 | bytes 28183536 | solution.py:46
  49.2 6.2 gather_fusion
  74.7 12.8 %scatter_fusion = f32[2048,256]{1,0:T(8,128)S(1)} fusion(f32[2048,256]{1,0:T(8,128)S(1)} %get-tuple-element.268, s32[1760]{0:T(1024)} %fusion.57, f32[1760,256]{1,0:T(8,128)} %reshape.372), kind=kCustom, calls=%fused_computation.10.clone.1 | custom fusion | flops 450560 | bytes 5413760 | tf_op jit(solution)/shard_map/while/body/eval_jaxpr/scatter-add | solution.py:40
  109.2 6.2 gather_fusion
  134.8 12.8 %scatter_fusion = f32[2048,256]{1,0:T(8,128)S(1)} fusion(f32[2048,256]{1,0:T(8,128)S(1)} %get-tuple-element.268, s32[1760]{0:T(1024)} %fusion.57, f32[1760,256]{1,0:T(8,128)} %reshape.372), kind=kCustom, calls=%fused_computation.10.clone.1 | custom fusion | flops 450560 | bytes 5413760 | tf_op jit(solution)/shard_map/while/body/eval_jaxpr/scatter-add | solution.py:40
  169.3 6.2 gather_fusion
  194.8 12.8 %scatter_fusion = f32[2048,256]{1,0:T(8,128)S(1)} fusion(f32[2048,256]{1,0:T(8,128)S(1)} %get-tuple-element.268, s32[1760]{0:T(1024)} %fusion.57, f32[1760,256]{1,0:T(8,128)} %reshape.372), kind=kCustom, calls=%fused_computation.10.clone.1 | custom fusion | flops 450560 | bytes 5413760 | tf_op jit(solution)/shard_map/while/body/eval_jaxpr/scatter-add | solution.py:40
  229.3 6.2 gather_fusion
  254.9 12.8 %scatter_fusion = f32[2048,256]{1,0:T(8,128)S(1)} fusion(f32[2048,256]{1,0:T(8,128)S(1)} %get-tuple-element.268, s32[1760]{0:T(1024)} %fusion.57, f32[1760,256]{1,0:T(8,128)} %reshape.372), kind=kCustom, calls=%fused_computation.10.clone.1 | custom fusion | flops 450560 | bytes 5413760 | tf_op jit(solution)/shard_map/while/body/eval_jaxpr/scatter-add | solution.py:40
  315.0 12.8 %scatter_fusion = f32[2048,256]{1,0:T(8,128)S(1)} fusion(f32[2048,256]{1,0:T(8,128)S(1)} %get-tuple-element.268, s32[1760]{0:T(1024)} %fusion.57, f32[1760,256]{1,0:T(8,128)} %reshape.372), kind=kCustom, calls=%fused_computation.10.clone.1 | custom fusion | flops 450560 | bytes 5413760 | tf_op jit(solution)/shard_map/while/body/eval_jaxpr/scatter-add | solution.py:40
  349.5 6.2 gather_fusion
  375.0 12.8 %scatter_fusion = f32[2048,256]{1,0:T(8,128)S(1)} fusion(f32[2048,256]{1,0:T(8,128)S(1)} %get-tuple-element.268, s32[1760]{0:T(1024)} %fusion.57, f32[1760,256]{1,0:T(8,128)} %reshape.372), kind=kCustom, calls=%fused_computation.10.clone.1 | custom fusion | flops 450560 | bytes 5413760 | tf_op jit(solution)/shard_map/while/body/eval_jaxpr/scatter-add | solution.py:40
  435.1 12.8 %scatter_fusion = f32[2048,256]{1,0:T(8,128)S(1)} fusion(f32[2048,256]{1,0:T(8,128)S(1)} %get-tuple-element.268, s32[1760]{0:T(1024)} %fusion.57, f32[1760,256]{1,0:T(8,128)} %reshape.372), kind=kCustom, calls=%fused_computation.10.clone.1 | custom fusion | flops 450560 | bytes 5413760 | tf_op jit(solution)/shard_map/while/body/eval_jaxpr/scatter-add | solution.py:40
  495.1 12.8 %scatter_fusion = f32[2048,256]{1,0:T(8,128)S(1)} fusion(f32[2048,256]{1,0:T(8,128)S(1)} %get-tuple-element.268, s32[1760]{0:T(1024)} %fusion.57, f32[1760,256]{1,0:T(8,128)} %reshape.372), kind=kCustom, calls=%fused_computation.10.clone.1 | custom fusion | flops 450560 | bytes 5413760 | tf_op jit(solution)/shard_map/while/body/eval_jaxpr/scatter-add | solution.py:40
  555.2 12.8 %scatter_fusion = f32[2048,256]{1,0:T(8,128)S(1)} fusion(f32[2048,256]{1,0:T(8,128)S(1)} %get-tuple-element.268, s32[1760]{0:T(1024)} %fusion.57, f32[1760,256]{1,0:T(8,128)} %reshape.372), kind=kCustom, calls=%fused_computation.10.clone.1 | custom fusion | flops 450560 | bytes 5413760 | tf_op jit(solution)/shard_map/while/body/eval_jaxpr/scatter-add | solution.py:40
  615.3 12.8 %scatter_fusion = f32[2048,256]{1,0:T(8,128)S(1)} fusion(f32[2048,256]{1,0:T(8,128)S(1)} %get-tuple-element.268, s32[1760]{0:T(1024)} %fusion.57, f32[1760,256]{1,0:T(8,128)} %reshape.372), kind=kCustom, calls=%fused_computation.10.clone.1 | custom fusion | flops 450560 | bytes 5413760 | tf_op jit(solution)/shard_map/while/body/eval_jaxpr/scatter-add | solution.py:40
  675.3 12.8 %scatter_fusion = f32[2048,256]{1,0:T(8,128)S(1)} fusion(f32[2048,256]{1,0:T(8,128)S(1)} %get-tuple-element.268, s32[1760]{0:T(1024)} %fusion.57, f32[1760,256]{1,0:T(8,128)} %reshape.372), kind=kCustom, calls=%fused_computation.10.clone.1 | custom fusion | flops 450560 | bytes 5413760 | tf_op jit(solution)/shard_map/while/body/eval_jaxpr/scatter-add | solution.py:40
  735.4 12.8 %scatter_fusion = f32[2048,256]{1,0:T(8,128)S(1)} fusion(f32[2048,256]{1,0:T(8,128)S(1)} %get-tuple-element.268, s32[1760]{0:T(1024)} %fusion.57, f32[1760,256]{1,0:T(8,128)} %reshape.372), kind=kCustom, calls=%fused_computation.10.clone.1 | custom fusion | flops 450560 | bytes 5413760 | tf_op jit(solution)/shard_map/while/body/eval_jaxpr/scatter-add | solution.py:40
  752.4 343.0 %while.21 = (s32[]{:T(128)}, f32[2048,512]{1,0:T(8,128)}, s32[6,16,110]{2,1,0:T(8,128)}, s32[6,16,110]{2,1,0:T(8,128)}, bf16[6,16,110]{2,1,0:T(8,128)(2,1)}, /*i...) while((s32[]{:T(128)}, f32[2048,512]{1,0:T(8,128)}, ...), condition=%wide.region_6.10_spmd, body=%wide.region_4.9_spmd.sunk | while | flops 1449722880 | bytes 43502576 | solution.py:46
  781.8 6.8 fusion.62
  792.2 17.3 %scatter_fusion.1 = f32[2048,512]{1,0:T(8,128)} fusion(f32[2048,512]{1,0:T(8,128)} %get-tuple-element.295, s32[1760]{0:T(1024)S(1)} %fusion.61, f32[1760,512]{1,0:T(8,128)} %reshape.384), kind=kCustom, calls=%fused_computation.11.clone.1 | custom fusion | flops 901120 | bytes 10820480 | tf_op jit(solution)/shard_map/while/body/eval_jaxpr/scatter-add | solution.py:40
  839.0 6.8 fusion.62
  849.4 17.3 %scatter_fusion.1 = f32[2048,512]{1,0:T(8,128)} fusion(f32[2048,512]{1,0:T(8,128)} %get-tuple-element.295, s32[1760]{0:T(1024)S(1)} %fusion.61, f32[1760,512]{1,0:T(8,128)} %reshape.384), kind=kCustom, calls=%fused_computation.11.clone.1 | custom fusion | flops 901120 | bytes 10820480 | tf_op jit(solution)/shard_map/while/body/eval_jaxpr/scatter-add | solution.py:40
  896.1 6.8 fusion.62
  906.6 17.3 %scatter_fusion.1 = f32[2048,512]{1,0:T(8,128)} fusion(f32[2048,512]{1,0:T(8,128)} %get-tuple-element.295, s32[1760]{0:T(1024)S(1)} %fusion.61, f32[1760,512]{1,0:T(8,128)} %reshape.384), kind=kCustom, calls=%fused_computation.11.clone.1 | custom fusion | flops 901120 | bytes 10820480 | tf_op jit(solution)/shard_map/while/body/eval_jaxpr/scatter-add | solution.py:40
  953.3 6.8 fusion.62
  963.7 17.3 %scatter_fusion.1 = f32[2048,512]{1,0:T(8,128)} fusion(f32[2048,512]{1,0:T(8,128)} %get-tuple-element.295, s32[1760]{0:T(1024)S(1)} %fusion.61, f32[1760,512]{1,0:T(8,128)} %reshape.384), kind=kCustom, calls=%fused_computation.11.clone.1 | custom fusion | flops 901120 | bytes 10820480 | tf_op jit(solution)/shard_map/while/body/eval_jaxpr/scatter-add | solution.py:40
  1010.5 6.8 fusion.62
  1020.9 17.3 %scatter_fusion.1 = f32[2048,512]{1,0:T(8,128)} fusion(f32[2048,512]{1,0:T(8,128)} %get-tuple-element.295, s32[1760]{0:T(1024)S(1)} %fusion.61, f32[1760,512]{1,0:T(8,128)} %reshape.384), kind=kCustom, calls=%fused_computation.11.clone.1 | custom fusion | flops 901120 | bytes 10820480 | tf_op jit(solution)/shard_map/while/body/eval_jaxpr/scatter-add | solution.py:40
  1067.6 6.8 fusion.62
  1078.1 17.3 %scatter_fusion.1 = f32[2048,512]{1,0:T(8,128)} fusion(f32[2048,512]{1,0:T(8,128)} %get-tuple-element.295, s32[1760]{0:T(1024)S(1)} %fusion.61, f32[1760,512]{1,0:T(8,128)} %reshape.384), kind=kCustom, calls=%fused_computation.11.clone.1 | custom fusion | flops 901120 | bytes 10820480 | tf_op jit(solution)/shard_map/while/body/eval_jaxpr/scatter-add | solution.py:40
  1100.9 89.3 %reduce-scatter.5.cloned.1.call-done = f32[256,512]{0,1:T(8,128)} async-done(((f32[2048,512]{0,1:T(8,128)}), f32[256,512]{0,1:T(8,128)}) %reduce-scatter.5.cloned.1.call-update) | async-done | bytes 524304 | tf_op jit(solution)/shard_map/reduce_scatter | solution.py:63
  (360 shorter events, 766.4 us)
Async XLA Ops:
  6.5 19.7 %all-gather.3.cloned.1.call-start = ((), (), s32[]{:S(2)}) async-start(), calls=%async_computation.2 | async-start | bytes 1310720 | tf_op jit(solution)/shard_map/all_gather | solution.py:58
  7.3 742.6 %all-gather.5.cloned.1.call-start = ((), (), s32[]{:S(2)}) async-start(), calls=%async_computation.4 | async-start | bytes 2359296 | tf_op jit(solution)/shard_map/all_gather | solution.py:59
  9.1 5.7 copy-start.4
  9.1 1091.8 %reduce-scatter.3.cloned.1.call-start = ((), (), s32[]{:S(2)}) async-start(), calls=%async_computation.3 | async-start | bytes 2621440 | tf_op jit(solution)/shard_map/reduce_scatter | solution.py:62
  14.8 1.7 copy-start.5
  17.5 8.9 copy-start
  26.2 1.2 copy-start.3
  748.2 1.4 copy-start.1
  749.6 440.5 %reduce-scatter.5.cloned.1.call-start = ((), (), s32[]{:S(2)}) async-start(), calls=%async_computation.5 | async-start | bytes 4718592 | tf_op jit(solution)/shard_map/reduce_scatter | solution.py:63
  749.9 2.5 copy-start.2
Sparse Core Ops, SparseCore 0:
  8.9 17.2 all-gather.2
  28.4 48.0 all-gather.4
  749.8 31.0 reduce-scatter.2
  1101.0 89.1 reduce-scatter.4
where the time goes:
time: 1210 us; the launch traced here: 1200 us
  local copies, waits for them, and re-layouts  595 us (49%)
  other arithmetic  397 us (33%)
  matrix products  97 us (8%)
  waiting for transfers between devices  95.1 us (8%)
  between operations  13.2 us (1%)
    gather x54, local copies, waits for them, and re-layouts, transform_block(): jnp.take(integrals, pair_ids, axis=0)  277 us
    scatter-add x18, other arithmetic, one_block(): partial_value.at[block_targets.reshape(-1)]  257 us
    gather x36, local copies, waits for them, and re-layouts, one_block(): rows = jnp.take(gathered, block_targets, axis=0)  155 us
    dot_general x18, matrix products, transform_block(): jnp.einsum('wen,wnl->wel', selector, transformed, preferred_element_type=...  97 us
    reduce_scatter x1, waiting for transfers between devices, on_device(): lax.psum_scatter(beta_terms, 'col', scatter_dimension=0, tiled=True)  89.3 us
    reshape x18, local copies, waits for them, and re-layouts, one_block(): picked.reshape(-1, width)  54.3 us
    mul x18, other arithmetic, transform_block(): jnp.take(integrals, pair_ids, axis=0)  49.4 us
  transfers between devices with their start and end apart: 4, of which 2 were waited for; matrix products, arithmetic and copies ran while one was open for 90% of the time, Pallas kernels for 0%

commit v1 on v0

v1 whole, which is shorter than its diff:
```python
import jax
import jax.numpy as jnp
from jax import lax
from jax.experimental import pallas as pl
from jax.experimental.pallas import tpu as pltpu
from jax.sharding import PartitionSpec as P

ORB = 20
GROUP = 16
EROW = 112
ELANE = 128


def hamiltonian_kernel(t_flat, p_row, s_row, cols, integrals_t, out, xs):
    step = pl.program_id(0)
    strings, width = out.shape
    norb2 = integrals_t.shape[0]

    rows_p = lax.broadcasted_iota(jnp.int32, (norb2, GROUP * ELANE), 0)
    pick = jnp.where(rows_p == p_row[0], s_row[0], 0.0).astype(jnp.bfloat16)
    a_t = jnp.dot(integrals_t[...], pick, preferred_element_type=jnp.float32).astype(jnp.bfloat16)
    lanes_n = lax.broadcasted_iota(jnp.int32, (EROW, norb2), 1)
    lanes_t = lax.broadcasted_iota(jnp.int32, (ELANE, width), 1)
    for i in range(GROUP):
        q_col = cols[0, 0, :EROW, i : i + 1]
        sign_col = cols[0, 1, :EROW, i : i + 1].astype(jnp.float32)
        t_col = cols[0, 2, :, i : i + 1]
        select = jnp.where(lanes_n == q_col, sign_col, 0.0).astype(jnp.bfloat16)
        g = jnp.dot(
            select, a_t[:, i * ELANE : (i + 1) * ELANE], preferred_element_type=jnp.float32
        ).astype(jnp.bfloat16)
        spread = jnp.where(lanes_t == t_col, 1.0, 0.0).astype(jnp.bfloat16)
        xs[i * EROW : (i + 1) * EROW, :] = jnp.dot(
            g, spread, preferred_element_type=jnp.float32
        ).astype(jnp.bfloat16)

    tile = 256
    t_all = t_flat[0]
    rows_j = lax.broadcasted_iota(jnp.int32, (tile, GROUP * EROW), 0).astype(jnp.bfloat16)

    @pl.when(step == 0)
    def _():
        out[...] = jnp.zeros_like(out)

    def one_tile(m, carry):
        local = jnp.clip(t_all - m * tile, -1, tile).astype(jnp.bfloat16)
        hot = jnp.where(rows_j == local, jnp.bfloat16(1.0), jnp.bfloat16(0.0))
        where = pl.ds(pl.multiple_of(m * tile, tile), tile)
        out[where, :] += jnp.dot(hot, xs[...], preferred_element_type=jnp.float32)
        return carry

    lax.fori_loop(0, strings // tile, one_tile, 0)


def same_spin_matrix(t, p, sign, offset, integrals_t, strings, width):
    windows, nex = t.shape
    groups = windows // GROUP
    q = p % ORB * ORB + p // ORB

    def padded(array, size, fill):
        return jnp.pad(array, ((0, 0), (0, size - nex)), constant_values=fill)

    t_flat = padded(t, EROW, -1).reshape(groups, 1, GROUP * EROW)
    p_row = padded(p, ELANE, -1).reshape(groups, 1, GROUP * ELANE)
    s_row = padded(sign, ELANE, 0).astype(jnp.float32).reshape(groups, 1, GROUP * ELANE)
    cols = jnp.stack([padded(q, ELANE, -1), padded(sign, ELANE, 0), padded(t - offset, ELANE, -1)])
    cols = cols.reshape(3, groups, GROUP, ELANE).transpose(1, 0, 3, 2)
    norb2 = integrals_t.shape[0]
    flops = 2 * strings * width * windows * EROW
    return pl.pallas_call(
        hamiltonian_kernel,
        grid=(groups,),
        in_specs=[
            pl.BlockSpec((1, 1, GROUP * EROW), lambda g: (g, 0, 0)),
            pl.BlockSpec((1, 1, GROUP * ELANE), lambda g: (g, 0, 0)),
            pl.BlockSpec((1, 1, GROUP * ELANE), lambda g: (g, 0, 0)),
            pl.BlockSpec((1, 3, ELANE, GROUP), lambda g: (g, 0, 0, 0)),
            pl.BlockSpec((norb2, norb2), lambda g: (0, 0)),
        ],
        out_specs=pl.BlockSpec((strings, width), lambda g: (0, 0)),
        out_shape=jax.ShapeDtypeStruct((strings, width), jnp.float32),
        scratch_shapes=[
            pltpu.VMEM((GROUP * EROW, width), jnp.bfloat16),
        ],
        compiler_params=pltpu.CompilerParams(vmem_limit_bytes=50 * 1024 * 1024),
        cost_estimate=pl.CostEstimate(
            flops=flops, bytes_accessed=strings * width * 4, transcendentals=0
        ),
    )(t_flat, p_row, s_row, cols, integrals_t)


def window_lists(targets, pairs, parity, window):
    nex, strings = targets.shape
    code = targets + pairs * 4096
    parts = jnp.concatenate(
        [code % 256, code // 256 % 256, code // 65536 + parity * 64], axis=0
    ).astype(jnp.bfloat16)
    hot = (window[:, None] == lax.broadcasted_iota(jnp.int32, (1, strings), 1)).astype(jnp.bfloat16)
    got = lax.dot_general(
        hot, parts, (((1,), (1,)), ((), ())), preferred_element_type=jnp.float32
    ).astype(jnp.int32)
    low, middle, high = got[:, :nex], got[:, nex : 2 * nex], got[:, 2 * nex :]
    code = low + middle * 256 + high % 64 * 65536
    return code % 4096, code // 4096, 1 - 2 * (high // 64)


def on_device(amplitudes, integrals, targets, pairs, parity, alpha_window, beta_window):
    rows, columns = amplitudes.shape
    strings = targets.shape[1]
    window = jnp.concatenate([alpha_window, beta_window])
    t, p, sign = window_lists(targets, pairs, parity, window)
    na = alpha_window.shape[0]
    alpha_columns = lax.all_gather(amplitudes, "row", axis=0, tiled=True)
    beta_columns = lax.all_gather(amplitudes, "col", axis=1, tiled=True)
    integrals_t = integrals.T
    beta_partial = same_spin_matrix(
        t[na:], p[na:], sign[na:], lax.axis_index("row") * rows, integrals_t, strings, rows
    )
    alpha_partial = same_spin_matrix(
        t[:na], p[:na], sign[:na], lax.axis_index("col") * columns, integrals_t, strings, columns
    )
    beta_own = lax.psum_scatter(beta_partial, "col", scatter_dimension=0, tiled=True)
    beta_all = lax.all_gather(beta_own.astype(jnp.bfloat16), "row", axis=1, tiled=True)
    alpha_own = lax.psum_scatter(alpha_partial, "row", scatter_dimension=0, tiled=True)
    alpha_all = lax.all_gather(alpha_own.astype(jnp.bfloat16), "col", axis=1, tiled=True)
    beta_part = lax.dot_general(
        beta_columns, beta_all, (((1,), (1,)), ((), ())), preferred_element_type=jnp.float32
    )
    alpha_part = jnp.dot(alpha_all, alpha_columns, preferred_element_type=jnp.float32)
    return alpha_part + beta_part


def solution(mesh):
    in_specs = (P("row", "col"), P(), P(), P(), P(), P("row"), P("col"))
    out_specs = P("row", "col")
    return jax.shard_map(
        on_device, mesh=mesh, in_specs=in_specs, out_specs=out_specs, check_vma=False
    )
```

time: 1210 us -> 345 us (0.29)
  local copies, waits for them, and re-layouts: 595 us -> 3.07 us
  other arithmetic: 397 us -> 8.48 us
  Pallas kernels: 0 us -> 139 us
  matrix products: 97 us -> 6.86 us
  waiting for transfers between devices: 95.1 us -> 168 us
    gather x96 -> x0, local copies, waits for them, and re-layouts: 436 us -> none  [the longest x54 277 us: transform_block(): jnp.take(integrals, pair_ids, axis=0)]
    scatter-add x18 -> x0, other arithmetic: 257 us -> none  [one_block(): partial_value.at[block_targets.reshape(-1)]]
    pallas_call x0 -> x2, Pallas kernels: none -> 139 us  [same_spin_matrix(): pl.pallas_call(hamiltonian_kernel, grid=(groups,), in_specs=[pl.BlockSpec...]
    all_gather x1 -> x3, waiting for transfers between devices: 0.02 us -> 119 us  [the longest x1 50.7 us: on_device(): lax.all_gather(alpha_own.astype(jnp.bfloat16), 'col', axis=1, tiled=True)]
    dot_general x18 -> x3, matrix products: 97 us -> 6.86 us  [the longest x1 3.36 us: on_device(): jnp.dot(alpha_all, alpha_columns, preferred_element_type=jnp.float32)]
    reshape x36 -> x2, local copies, waits for them, and re-layouts: 71.4 us -> 0.3 us  [same_spin_matrix(): t_flat = padded(t, EROW, -1).reshape(groups, 1, GROUP * EROW)]
    reduce_scatter x2, waiting for transfers between devices: 89.3 us -> 32.9 us  [the longest x1 30.5 us: on_device(): lax.psum_scatter(alpha_partial, 'row', scatter_dimension=0, tiled=True)]
    mul x18 -> x0, other arithmetic: 49.4 us -> none  [transform_block(): jnp.take(integrals, pair_ids, axis=0)]
  transfers between devices with their start and end apart: 4 -> 6, of which waited for: 2 -> 6; matrix products, arithmetic and copies ran while one was open for 90% -> 3% of each run, Pallas kernels for 0% -> 25%
where the time goes in v1:
time: 345 us; the launch traced here: 340 us
  waiting for transfers between devices  168 us (49%)
  Pallas kernels  139 us (40%)
  between operations  13.7 us (4%)
  other arithmetic  8.48 us (2%)
  matrix products  6.86 us (2%)
    pallas_call x2, Pallas kernels, same_spin_matrix(): pl.pallas_call(hamiltonian_kernel, grid=(groups,), in_specs=[pl.BlockSpec...  139 us
    all_gather x1, waiting for transfers between devices, on_device(): lax.all_gather(alpha_own.astype(jnp.bfloat16), 'col', axis=1, tiled=True)  50.7 us
    all_gather x1, waiting for transfers between devices, on_device(): beta_columns = lax.all_gather(amplitudes, 'col', axis=1, tiled=True)  49.4 us
    reduce_scatter x1, waiting for transfers between devices, on_device(): lax.psum_scatter(alpha_partial, 'row', scatter_dimension=0, tiled=True)  30.5 us
    all_gather x1, waiting for transfers between devices, on_device(): lax.all_gather(beta_own.astype(jnp.bfloat16), 'row', axis=1, tiled=True)  18.7 us
    all_gather x1, waiting for transfers between devices, on_device(): alpha_columns = lax.all_gather(amplitudes, 'row', axis=0, tiled=True)  15.5 us
  transfers between devices with their start and end apart: 6, of which 6 were waited for; matrix products, arithmetic and copies ran while one was open for 3% of the time, Pallas kernels for 25%

profile of v1, /device:TPU:15, one launch (start us, length us, event | category | flops | bytes accessed | tf_op | source)
XLA Modules:
  0.0 340.3 jit_solution(4593951687482986701)
XLA Ops:
  6.5 0.8 pad_add_fusion.2
  7.3 3.4 %fusion.10 = (bf16[110,2048]{1,0:T(8,128)(2,1)S(1)}, bf16[110,2048]{1,0:T(8,128)(2,1)S(1)}, bf16[110,2048]{1,0:T(8,128)(2,1)S(1)}) fusion(s32[110,2048]{1,0:T(8,128)} %param.9, s32[110,2048]{1,0:T(8,128)} %param.10, s32[110,2048]{1,0:T(8,128)} %param.11), kind=kLoop, calls=%fused_computation.22 | loop fusion | flops 10588160 | bytes 4055040 | tf_op jit(solution)/shard_map/convert
  10.7 0.8 fusion.6
  11.6 0.2 fusion.21
  11.8 0.2 add_select_fusion.5
  12.0 0.1 add_select_fusion.6
  12.1 0.1 reshape.36.t_flat
  12.3 0.1 fusion.31
  12.4 0.4 copy.20
  12.8 0.2 copy.19
  13.0 56.1 %shard_map.74 = f32[2048,512]{1,0:T(8,128)} custom-call(s32[6,1,1792]{2,1,0:T(1,128)S(1)} %reshape.36.t_flat, s32[6,1,2048]{2,1,0:T(1,128)S(1)} %bitcast.24, f32[6,1,2048]{2,1,0:T(1,128)S(1)} %bitcast.25, s32[6,3,128,16]{3,2,1,0:T(8,128)S(1)} %bitcast.19, bf16[400,400]{1,0:T(8,128)(2,1)S(1)} %bitcast.20), custom_call_target="tpu_custom_call" | custom-call | flops 22548578304 | bytes 4194304 | tf_op jit(solution)/shard_map/pallas_call | solution.py:70
  69.1 0.0 reduce-scatter.3.cloned.1.call-start
  69.2 0.2 reshape.33.t_flat
  69.4 0.1 fusion.26
  69.6 2.1 copy.18
  71.7 83.4 %shard_map.73 = f32[2048,256]{1,0:T(8,128)} custom-call(s32[12,1,1792]{2,1,0:T(1,128)S(1)} %reshape.33.t_flat, s32[12,1,2048]{2,1,0:T(1,128)S(1)} %bitcast.22, f32[12,1,2048]{2,1,0:T(1,128)S(1)} %bitcast.23, s32[12,3,128,16]{3,2,1,0:T(8,128)} %bitcast.26, bf16[400,400]{1,0:T(8,128)(2,1)S(1)} %bitcast.21), custom_call_target="tpu_custom_call" | custom-call | flops 22548578304 | bytes 2097152 | tf_op jit(solution)/shard_map/pallas_call | solution.py:70
  155.2 0.0 all-gather.11.cloned.1.call-start
  155.2 0.7 all-gather.11.cloned.1.call-update
  155.9 0.0 all-gather.9.cloned.1.call-start
  155.9 2.4 reduce-scatter.5.cloned.1.call-done
  158.4 1.8 convert_element_type.21
  160.2 0.0 all-gather.7.cloned.1.call-start
  160.2 0.5 all-gather.7.cloned.1.call-update
  160.8 0.0 all-gather.5.cloned.1.call-start
  160.8 30.5 %reduce-scatter.3.cloned.1.call-done = f32[512,256]{1,0:T(8,128)} async-done(((f32[2048,256]{1,0:T(8,128)}), f32[512,256]{1,0:T(8,128)}) %reduce-scatter.3.cloned.1.call-update) | async-done | bytes 524304 | tf_op jit(solution)/shard_map/reduce_scatter | solution.py:124
  191.3 1.8 convert_element_type.19
  193.1 49.4 %all-gather.11.cloned.1.call-done = bf16[512,2048]{1,0:T(8,128)(2,1)} async-done(((bf16[512,256]{1,0:T(8,128)(2,1)}), bf16[512,2048]{1,0:T(8,128)(2,1)}) %all-gather.11.cloned.1.call-update) | async-done | bytes 2097168 | tf_op jit(solution)/shard_map/all_gather | solution.py:114
  242.5 18.7 %all-gather.9.cloned.1.call-done = bf16[256,2048]{1,0:T(8,128)(2,1)} async-done(((bf16[256,512]{1,0:T(8,128)(2,1)}), bf16[256,2048]{1,0:T(8,128)(2,1)}) %all-gather.9.cloned.1.call-update) | async-done | bytes 1048592 | tf_op jit(solution)/shard_map/all_gather | solution.py:123
  261.2 2.7 convolution_bitcast_fusion
  263.9 15.5 %all-gather.7.cloned.1.call-done = bf16[2048,256]{1,0:T(8,128)(2,1)} async-done(((bf16[512,256]{1,0:T(8,128)(2,1)}), bf16[2048,256]{1,0:T(8,128)(2,1)}) %all-gather.7.cloned.1.call-update) | async-done | bytes 1048592 | tf_op jit(solution)/shard_map/all_gather | solution.py:113
  279.4 50.7 %all-gather.5.cloned.1.call-done = bf16[512,2048]{1,0:T(8,128)(2,1)} async-done(((bf16[512,256]{1,0:T(8,128)(2,1)}), bf16[512,2048]{1,0:T(8,128)(2,1)}) %all-gather.5.cloned.1.call-update) | async-done | bytes 2097168 | tf_op jit(solution)/shard_map/all_gather | solution.py:125
  330.0 3.4 convolution_add_fusion
  (23 shorter events, 0.2 us)
Async XLA Ops:
  6.5 151.8 %reduce-scatter.5.cloned.1.call-start = ((), (), s32[]{:S(2)}) async-start(), calls=%async_computation.5 | async-start | bytes 4718592 | tf_op jit(solution)/shard_map/reduce_scatter | solution.py:122
  11.6 1.2 copy-start
  69.1 122.2 %reduce-scatter.3.cloned.1.call-start = ((), (), s32[]{:S(2)}) async-start(), calls=%async_computation.2 | async-start | bytes 2621440 | tf_op jit(solution)/shard_map/reduce_scatter | solution.py:124
  155.2 87.4 %all-gather.11.cloned.1.call-start = ((), (), s32[]{:S(2)}) async-start(), calls=%async_computation.7 | async-start | bytes 2359296 | tf_op jit(solution)/shard_map/all_gather | solution.py:114
  155.9 105.3 %all-gather.9.cloned.1.call-start = ((), (), s32[]{:S(2)}) async-start(), calls=%async_computation.6 | async-start | bytes 1310720 | tf_op jit(solution)/shard_map/all_gather | solution.py:123
  160.2 119.2 %all-gather.7.cloned.1.call-start = ((), (), s32[]{:S(2)}) async-start(), calls=%async_computation.4 | async-start | bytes 1310720 | tf_op jit(solution)/shard_map/all_gather | solution.py:113
  160.8 169.3 %all-gather.5.cloned.1.call-start = ((), (), s32[]{:S(2)}) async-start(), calls=%async_computation.3 | async-start | bytes 2359296 | tf_op jit(solution)/shard_map/all_gather | solution.py:125
Sparse Core Ops, SparseCore 0:
  69.2 89.1 reduce-scatter.4
  161.0 30.1 reduce-scatter.2
  193.3 49.1 all-gather.10
  243.9 17.2 all-gather.8
  262.6 16.7 all-gather.6
  281.3 48.7 all-gather.4

commit v2 on v1

--- a/solution.py
+++ b/solution.py
@@ -21,17 +21,21 @@
     a_t = jnp.dot(integrals_t[...], pick, preferred_element_type=jnp.float32).astype(jnp.bfloat16)
     lanes_n = lax.broadcasted_iota(jnp.int32, (EROW, norb2), 1)
     lanes_t = lax.broadcasted_iota(jnp.int32, (ELANE, width), 1)
+    gs = []
     for i in range(GROUP):
         q_col = cols[0, 0, :EROW, i : i + 1]
         sign_col = cols[0, 1, :EROW, i : i + 1].astype(jnp.float32)
+        select = jnp.where(lanes_n == q_col, sign_col, 0.0).astype(jnp.bfloat16)
+        gs.append(
+            jnp.dot(
+                select, a_t[:, i * ELANE : (i + 1) * ELANE], preferred_element_type=jnp.float32
+            ).astype(jnp.bfloat16)
+        )
+    for i in range(GROUP):
         t_col = cols[0, 2, :, i : i + 1]
-        select = jnp.where(lanes_n == q_col, sign_col, 0.0).astype(jnp.bfloat16)
-        g = jnp.dot(
-            select, a_t[:, i * ELANE : (i + 1) * ELANE], preferred_element_type=jnp.float32
-        ).astype(jnp.bfloat16)
         spread = jnp.where(lanes_t == t_col, 1.0, 0.0).astype(jnp.bfloat16)
         xs[i * EROW : (i + 1) * EROW, :] = jnp.dot(
-            g, spread, preferred_element_type=jnp.float32
+            gs[i], spread, preferred_element_type=jnp.float32
         ).astype(jnp.bfloat16)
 
     tile = 256
@@ -104,30 +108,54 @@
     return code % 4096, code // 4096, 1 - 2 * (high // 64)
 
 
+def shifted(block, axis_name):
+    n = lax.axis_size(axis_name)
+    blocks = [block]
+    for k in range(1, n):
+        blocks.append(lax.ppermute(block, axis_name, [((i + k) % n, i) for i in range(n)]))
+    return blocks
+
+
+def in_order(blocks, axis_name, dim):
+    n, size = len(blocks), blocks[0].shape[dim]
+    twice = jnp.concatenate(blocks + blocks, axis=dim)
+    start = (n - lax.axis_index(axis_name)) * size
+    return lax.dynamic_slice_in_dim(twice, start, n * size, axis=dim)
+
+
 def on_device(amplitudes, integrals, targets, pairs, parity, alpha_window, beta_window):
     rows, columns = amplitudes.shape
     strings = targets.shape[1]
     window = jnp.concatenate([alpha_window, beta_window])
     t, p, sign = window_lists(targets, pairs, parity, window)
     na = alpha_window.shape[0]
-    alpha_columns = lax.all_gather(amplitudes, "row", axis=0, tiled=True)
-    beta_columns = lax.all_gather(amplitudes, "col", axis=1, tiled=True)
+    row, col = lax.axis_index("row"), lax.axis_index("col")
+    n_row, n_col = lax.axis_size("row"), lax.axis_size("col")
+    row_blocks = shifted(amplitudes, "row")
+    col_blocks = shifted(amplitudes, "col")
     integrals_t = integrals.T
     beta_partial = same_spin_matrix(
-        t[na:], p[na:], sign[na:], lax.axis_index("row") * rows, integrals_t, strings, rows
-    )
-    alpha_partial = same_spin_matrix(
-        t[:na], p[:na], sign[:na], lax.axis_index("col") * columns, integrals_t, strings, columns
+        t[na:], p[na:], sign[na:], row * rows, integrals_t, strings, rows
     )
     beta_own = lax.psum_scatter(beta_partial, "col", scatter_dimension=0, tiled=True)
-    beta_all = lax.all_gather(beta_own.astype(jnp.bfloat16), "row", axis=1, tiled=True)
+    alpha_partial = same_spin_matrix(
+        t[:na], p[:na], sign[:na], col * columns, integrals_t, strings, columns
+    )
     alpha_own = lax.psum_scatter(alpha_partial, "row", scatter_dimension=0, tiled=True)
-    alpha_all = lax.all_gather(alpha_own.astype(jnp.bfloat16), "col", axis=1, tiled=True)
-    beta_part = lax.dot_general(
-        beta_columns, beta_all, (((1,), (1,)), ((), ())), preferred_element_type=jnp.float32
-    )
-    alpha_part = jnp.dot(alpha_all, alpha_columns, preferred_element_type=jnp.float32)
-    return alpha_part + beta_part
+    alpha_columns = in_order(row_blocks, "row", 0)
+    beta_columns = in_order(col_blocks, "col", 1)
+    total = jnp.zeros((rows, columns), jnp.float32)
+    for k, block in enumerate(shifted(beta_own.astype(jnp.bfloat16), "row")):
+        start = (row + k) % n_row * rows
+        part = lax.dynamic_slice_in_dim(beta_columns, start, rows, axis=1)
+        total += lax.dot_general(
+            part, block, (((1,), (1,)), ((), ())), preferred_element_type=jnp.float32
+        )
+    for k, block in enumerate(shifted(alpha_own.astype(jnp.bfloat16), "col")):
+        start = (col + k) % n_col * columns
+        part = lax.dynamic_slice_in_dim(alpha_columns, start, columns, axis=0)
+        total += jnp.dot(block, part, preferred_element_type=jnp.float32)
+    return total
 
 
 def solution(mesh):

time: 345 us -> 318 us (0.922); the launches traced: 340 us -> 317 us
  waiting for transfers between devices: 168 us -> 104 us
  starting transfers between devices: 0.2 us -> 43.7 us
  Pallas kernels: 139 us -> 110 us
  local copies, waits for them, and re-layouts: 3.07 us -> 21.2 us
  matrix products: 6.86 us -> 16.9 us
    all_gather x4 -> x0, waiting for transfers between devices: 134 us -> none  [the longest x1 50.7 us: on_device(): lax.all_gather(alpha_own.astype(jnp.bfloat16), 'col', axis=1, tiled=True)]
    ppermute x0 -> x20, waiting for transfers between devices: none -> 104 us  [shifted(): lax.ppermute(block, axis_name, [((i + k) % n, i) for i in range(n)])]
    ppermute x0 -> x20, starting transfers between devices: none -> 43.6 us  [shifted(): lax.ppermute(block, axis_name, [((i + k) % n, i) for i in range(n)])]
    reduce_scatter x1, waiting for transfers between devices: 30.5 us -> 0.01 us  [on_device(): lax.psum_scatter(alpha_partial, 'row', scatter_dimension=0, tiled=True)]
    pallas_call x2, Pallas kernels: 139 us -> 110 us  [same_spin_matrix(): pl.pallas_call(hamiltonian_kernel, grid=(groups,), in_specs=[pl.BlockSpec...]
    unnamed x3 -> x26, local copies, waits for them, and re-layouts: 0.18 us -> 16.8 us
    dot_general x2 -> x12, matrix products: 6.02 us -> 16.1 us  [the longest x8 9.2 us: on_device(): total += jnp.dot(block, part, preferred_element_type=jnp.float32)]
  transfers between devices with their start and end apart: 6 -> 22, of which waited for: 6 -> 12; matrix products, arithmetic and copies ran while one was open for 3% -> 10% of each run, Pallas kernels for 25% -> 14%
where the time goes in v2:
time: 318 us; the launch traced here: 317 us
  Pallas kernels  110 us (35%)
  waiting for transfers between devices  104 us (33%)
  starting transfers between devices  43.7 us (14%)
  local copies, waits for them, and re-layouts  21.2 us (7%)
  matrix products  16.9 us (5%)
  between operations  13.8 us (4%)
  other arithmetic  7.76 us (2%)
    pallas_call x2, Pallas kernels, same_spin_matrix(): pl.pallas_call(hamiltonian_kernel, grid=(groups,), in_specs=[pl.BlockSpec...  110 us
    ppermute x20, waiting for transfers between devices, shifted(): lax.ppermute(block, axis_name, [((i + k) % n, i) for i in range(n)])  104 us
    ppermute x20, starting transfers between devices, shifted(): lax.ppermute(block, axis_name, [((i + k) % n, i) for i in range(n)])  43.6 us
    unnamed x26, local copies, waits for them, and re-layouts  16.8 us
    dot_general x8, matrix products, on_device(): total += jnp.dot(block, part, preferred_element_type=jnp.float32)  9.2 us
    dot_general x4, matrix products, on_device(): lax.dot_general(part, block, (((1,), (1,)), ((), ())), preferred_element_...  6.87 us
  transfers between devices with their start and end apart: 22, of which 12 were waited for; matrix products, arithmetic and copies ran while one was open for 10% of the time, Pallas kernels for 14%

profile of v2, /device:TPU:15, one launch (start us, length us, event | category | flops | bytes accessed | tf_op | source)
XLA Modules:
  0.0 317.5 jit_solution(11080804026582319836)
XLA Ops:
  7.3 3.4 %fusion.20 = (bf16[110,2048]{1,0:T(8,128)(2,1)S(1)}, bf16[110,2048]{1,0:T(8,128)(2,1)S(1)}, bf16[110,2048]{1,0:T(8,128)(2,1)S(1)}) fusion(s32[110,2048]{1,0:T(8,128)} %param.9, s32[110,2048]{1,0:T(8,128)} %param.10, s32[110,2048]{1,0:T(8,128)} %param.11), kind=kLoop, calls=%fused_computation.31 | loop fusion | flops 10588160 | bytes 4055040 | tf_op jit(solution)/shard_map/convert
  12.5 2.1 copy.18
  14.8 64.6 %shard_map.74 = f32[2048,256]{1,0:T(8,128)} custom-call(s32[12,1,1792]{2,1,0:T(1,128)S(1)} %reshape.36.t_flat, s32[12,1,2048]{2,1,0:T(1,128)S(1)} %bitcast.28, f32[12,1,2048]{2,1,0:T(1,128)S(1)} %bitcast.29, s32[12,3,128,16]{3,2,1,0:T(8,128)} %bitcast.32, bf16[400,400]{1,0:T(8,128)(2,1)S(1)} %bitcast.26), custom_call_target="tpu_custom_call" | custom-call | flops 22548578304 | bytes 2097152 | tf_op jit(solution)/shard_map/pallas_call | solution.py:74
  80.2 45.3 %shard_map.73 = f32[2048,512]{1,0:T(8,128)} custom-call(s32[6,1,1792]{2,1,0:T(1,128)S(1)} %reshape.33.t_flat, s32[6,1,2048]{2,1,0:T(1,128)S(1)} %bitcast.30, f32[6,1,2048]{2,1,0:T(1,128)S(1)} %bitcast.31, s32[6,3,128,16]{3,2,1,0:T(8,128)S(1)} %bitcast.25, bf16[400,400]{1,0:T(8,128)(2,1)S(1)} %bitcast.27), custom_call_target="tpu_custom_call" | custom-call | flops 22548578304 | bytes 4194304 | tf_op jit(solution)/shard_map/pallas_call | solution.py:74
  126.8 4.1 %collective-permute-start.2 = (bf16[512,256]{1,0:T(8,128)(2,1)S(1)}, bf16[512,256]{1,0:T(8,128)(2,1)S(1)}, u32[]{:S(2)}, u32[]{:S(2)}) collective-permute-start(bf16[512,256]{1,0:T(8,128)(2,1)S(1)} %copy-done), channel_id=1, source_target_pairs={{3,0},{4,1},{5,2},{6,3},{7,4},{0,5},{1,6},{2,7},{11,8},{12,9},{13,... | collective-permute-start | bytes 786440 | tf_op jit(solution)/shard_map/ppermute | solution.py:115
  131.0 2.2 collective-permute-start.4
  134.5 1.3 collective-permute-start.5
  136.5 8.8 %collective-permute-start.6 = (bf16[512,256]{1,0:T(8,128)(2,1)S(1)}, bf16[512,256]{1,0:T(8,128)(2,1)S(1)}, u32[]{:S(2)}, u32[]{:S(2)}) collective-permute-start(bf16[512,256]{1,0:T(8,128)(2,1)S(1)} %copy-done), channel_id=1, source_target_pairs={{7,0},{0,1},{1,2},{2,3},{3,4},{4,5},{5,6},{6,7},{15,8},{8,9},{9,10... | collective-permute-start | bytes 786440 | tf_op jit(solution)/shard_map/ppermute | solution.py:115
  146.1 9.0 %collective-permute-done.2 = bf16[512,256]{1,0:T(8,128)(2,1)S(1)} collective-permute-done((bf16[512,256]{1,0:T(8,128)(2,1)S(1)}, bf16[512,256]{1,0:T(8,128)(2,1)S(1)}, u32[]{:S(2)}, u32[]{:S(2)}) %collective-permute-start.2) | collective-permute-done | bytes 262176 | tf_op jit(solution)/shard_map/ppermute | solution.py:115
  155.2 11.7 %collective-permute-start.10 = (bf16[512,256]{1,0:T(8,128)(2,1)S(1)}, bf16[512,256]{1,0:T(8,128)(2,1)S(1)}, u32[]{:S(2)}, u32[]{:S(2)}) collective-permute-start(bf16[512,256]{1,0:T(8,128)(2,1)S(1)} %copy-done), channel_id=1, source_target_pairs={{8,0},{16,8},{24,16},{0,24},{9,1},{17,9},{25,17},{1,25},{10,2},{18... | collective-permute-start | bytes 786440 | tf_op jit(solution)/shard_map/ppermute | solution.py:115
  167.6 4.0 %collective-permute-done.3 = bf16[512,256]{1,0:T(8,128)(2,1)S(1)} collective-permute-done((bf16[512,256]{1,0:T(8,128)(2,1)S(1)}, bf16[512,256]{1,0:T(8,128)(2,1)S(1)}, u32[]{:S(2)}, u32[]{:S(2)}) %collective-permute-start.3) | collective-permute-done | bytes 262176 | tf_op jit(solution)/shard_map/ppermute | solution.py:115
  172.5 11.7 %collective-permute-done.4 = bf16[512,256]{1,0:T(8,128)(2,1)S(1)} collective-permute-done((bf16[512,256]{1,0:T(8,128)(2,1)S(1)}, bf16[512,256]{1,0:T(8,128)(2,1)S(1)}, u32[]{:S(2)}, u32[]{:S(2)}) %collective-permute-start.4) | collective-permute-done | bytes 262176 | tf_op jit(solution)/shard_map/ppermute | solution.py:115
  185.5 12.2 %collective-permute-done.5 = bf16[512,256]{1,0:T(8,128)(2,1)S(1)} collective-permute-done((bf16[512,256]{1,0:T(8,128)(2,1)S(1)}, bf16[512,256]{1,0:T(8,128)(2,1)S(1)}, u32[]{:S(2)}, u32[]{:S(2)}) %collective-permute-start.5) | collective-permute-done | bytes 262176 | tf_op jit(solution)/shard_map/ppermute | solution.py:115
  198.4 10.5 %collective-permute-done.6 = bf16[512,256]{1,0:T(8,128)(2,1)S(1)} collective-permute-done((bf16[512,256]{1,0:T(8,128)(2,1)S(1)}, bf16[512,256]{1,0:T(8,128)(2,1)S(1)}, u32[]{:S(2)}, u32[]{:S(2)}) %collective-permute-start.6) | collective-permute-done | bytes 262176 | tf_op jit(solution)/shard_map/ppermute | solution.py:115
  220.3 1.8 convert_element_type.21
  222.8 3.7 %collective-permute-start.16 = (bf16[512,256]{1,0:T(8,128)(2,1)}, bf16[512,256]{1,0:T(8,128)(2,1)S(1)}, u32[]{:S(2)}, u32[]{:S(2)}) collective-permute-start(bf16[512,256]{1,0:T(8,128)(2,1)} %convert_element_type.21), channel_id=1, source_target_pairs={{4,0},{5,1},{6,2},{7,3},{0,4},{1,5},{2,6},{3,7},{12,8},{13,9},{14,... | collective-permute-start | bytes 786440 | tf_op jit(solution)/shard_map/ppermute | solution.py:115
  226.5 1.5 collective-permute-start.15
  228.0 2.4 collective-permute-start.14
  230.4 1.2 collective-permute-start.13
  231.5 1.2 fusion.56
  232.8 9.4 %collective-permute-done.17 = bf16[512,256]{1,0:T(8,128)(2,1)S(1)} collective-permute-done((bf16[512,256]{1,0:T(8,128)(2,1)}, bf16[512,256]{1,0:T(8,128)(2,1)S(1)}, u32[]{:S(2)}, u32[]{:S(2)}) %collective-permute-start.17) | collective-permute-done | bytes 262176 | tf_op jit(solution)/shard_map/ppermute | solution.py:115
  242.1 3.4 %collective-permute-start.18 = (bf16[512,256]{1,0:T(8,128)(2,1)}, bf16[512,256]{1,0:T(8,128)(2,1)}, u32[]{:S(2)}, u32[]{:S(2)}) collective-permute-start(bf16[512,256]{1,0:T(8,128)(2,1)} %convert_element_type.21), channel_id=1, source_target_pairs={{6,0},{7,1},{0,2},{1,3},{2,4},{3,5},{4,6},{5,7},{14,8},{15,9},{8,1... | collective-permute-start | bytes 786440 | tf_op jit(solution)/shard_map/ppermute | solution.py:115
  246.7 20.5 %collective-permute-done.16 = bf16[512,256]{1,0:T(8,128)(2,1)S(1)} collective-permute-done((bf16[512,256]{1,0:T(8,128)(2,1)}, bf16[512,256]{1,0:T(8,128)(2,1)S(1)}, u32[]{:S(2)}, u32[]{:S(2)}) %collective-permute-start.16) | collective-permute-done | bytes 262176 | tf_op jit(solution)/shard_map/ppermute | solution.py:115
  268.4 1.1 fusion.50
  269.5 19.7 %collective-permute-done.14 = bf16[512,256]{1,0:T(8,128)(2,1)S(1)} collective-permute-done((bf16[512,256]{1,0:T(8,128)(2,1)}, bf16[512,256]{1,0:T(8,128)(2,1)S(1)}, u32[]{:S(2)}, u32[]{:S(2)}) %collective-permute-start.14) | collective-permute-done | bytes 262176 | tf_op jit(solution)/shard_map/ppermute | solution.py:115
  293.0 1.2 fusion.44
  294.2 1.5 collective-permute-start.8
  297.2 1.5 fusion.28
  298.7 6.0 %collective-permute-done.8 = bf16[256,512]{1,0:T(8,128)(2,1)S(1)} collective-permute-done((bf16[256,512]{1,0:T(8,128)(2,1)S(1)}, bf16[256,512]{1,0:T(8,128)(2,1)S(1)}, u32[]{:S(2)}, u32[]{:S(2)}) %collective-permute-start.8) | collective-permute-done | bytes 262176 | tf_op jit(solution)/shard_map/ppermute | solution.py:115
  304.7 1.5 fusion.30
  306.7 1.5 fusion.32
  308.1 2.5 fusion.15
  (86 shorter events, 31.3 us)
Async XLA Ops:
  6.5 213.8 %reduce-scatter.5.cloned.1.call-start = ((), (), s32[]{:S(2)}) async-start(), calls=%async_computation.3 | async-start | bytes 2621440 | tf_op jit(solution)/shard_map/reduce_scatter | solution.py:144
  10.7 1.4 copy-start.1
  79.4 212.1 %reduce-scatter.3.cloned.1.call-start = ((), (), s32[]{:S(2)}) async-start(), calls=%async_computation.2 | async-start | bytes 4718592 | tf_op jit(solution)/shard_map/reduce_scatter | solution.py:140
  125.5 0.9 copy-start
  126.4 8.1 %collective-permute-start = (bf16[512,256]{1,0:T(8,128)(2,1)S(1)}, bf16[512,256]{1,0:T(8,128)(2,1)S(1)}, u32[]{:S(2)}, u32[]{:S(2)}) collective-permute-start(bf16[512,256]{1,0:T(8,128)(2,1)S(1)} %copy-done), channel_id=1, source_target_pairs={{1,0},{2,1},{3,2},{4,3},{5,4},{6,5},{7,6},{0,7},{9,8},{10,9},{11,1... | collective-permute-start | bytes 786440 | tf_op jit(solution)/shard_map/ppermute | solution.py:115
  126.7 9.9 %collective-permute-start.1 = (bf16[512,256]{1,0:T(8,128)(2,1)S(1)}, bf16[512,256]{1,0:T(8,128)(2,1)S(1)}, u32[]{:S(2)}, u32[]{:S(2)}) collective-permute-start(bf16[512,256]{1,0:T(8,128)(2,1)S(1)} %copy-done), channel_id=1, source_target_pairs={{2,0},{3,1},{4,2},{5,3},{6,4},{7,5},{0,6},{1,7},{10,8},{11,9},{12,... | collective-permute-start | bytes 786440 | tf_op jit(solution)/shard_map/ppermute | solution.py:115
  126.8 28.3 %collective-permute-start.2 = (bf16[512,256]{1,0:T(8,128)(2,1)S(1)}, bf16[512,256]{1,0:T(8,128)(2,1)S(1)}, u32[]{:S(2)}, u32[]{:S(2)}) collective-permute-start(bf16[512,256]{1,0:T(8,128)(2,1)S(1)} %copy-done), channel_id=1, source_target_pairs={{3,0},{4,1},{5,2},{6,3},{7,4},{0,5},{1,6},{2,7},{11,8},{12,9},{13,... | collective-permute-start | bytes 786440 | tf_op jit(solution)/shard_map/ppermute | solution.py:115
  131.0 40.6 %collective-permute-start.3 = (bf16[512,256]{1,0:T(8,128)(2,1)S(1)}, bf16[512,256]{1,0:T(8,128)(2,1)S(1)}, u32[]{:S(2)}, u32[]{:S(2)}) collective-permute-start(bf16[512,256]{1,0:T(8,128)(2,1)S(1)} %copy-done), channel_id=1, source_target_pairs={{4,0},{5,1},{6,2},{7,3},{0,4},{1,5},{2,6},{3,7},{12,8},{13,9},{14,... | collective-permute-start | bytes 786440 | tf_op jit(solution)/shard_map/ppermute | solution.py:115
  131.0 53.2 %collective-permute-start.4 = (bf16[512,256]{1,0:T(8,128)(2,1)S(1)}, bf16[512,256]{1,0:T(8,128)(2,1)S(1)}, u32[]{:S(2)}, u32[]{:S(2)}) collective-permute-start(bf16[512,256]{1,0:T(8,128)(2,1)S(1)} %copy-done), channel_id=1, source_target_pairs={{5,0},{6,1},{7,2},{0,3},{1,4},{2,5},{3,6},{4,7},{13,8},{14,9},{15,... | collective-permute-start | bytes 786440 | tf_op jit(solution)/shard_map/ppermute | solution.py:115
  134.5 63.2 %collective-permute-start.5 = (bf16[512,256]{1,0:T(8,128)(2,1)S(1)}, bf16[512,256]{1,0:T(8,128)(2,1)S(1)}, u32[]{:S(2)}, u32[]{:S(2)}) collective-permute-start(bf16[512,256]{1,0:T(8,128)(2,1)S(1)} %copy-done), channel_id=1, source_target_pairs={{6,0},{7,1},{0,2},{1,3},{2,4},{3,5},{4,6},{5,7},{14,8},{15,9},{8,1... | collective-permute-start | bytes 786440 | tf_op jit(solution)/shard_map/ppermute | solution.py:115
  136.5 72.4 %collective-permute-start.6 = (bf16[512,256]{1,0:T(8,128)(2,1)S(1)}, bf16[512,256]{1,0:T(8,128)(2,1)S(1)}, u32[]{:S(2)}, u32[]{:S(2)}) collective-permute-start(bf16[512,256]{1,0:T(8,128)(2,1)S(1)} %copy-done), channel_id=1, source_target_pairs={{7,0},{0,1},{1,2},{2,3},{3,4},{4,5},{5,6},{6,7},{15,8},{8,9},{9,10... | collective-permute-start | bytes 786440 | tf_op jit(solution)/shard_map/ppermute | solution.py:115
  155.2 55.4 %collective-permute-start.10 = (bf16[512,256]{1,0:T(8,128)(2,1)S(1)}, bf16[512,256]{1,0:T(8,128)(2,1)S(1)}, u32[]{:S(2)}, u32[]{:S(2)}) collective-permute-start(bf16[512,256]{1,0:T(8,128)(2,1)S(1)} %copy-done), channel_id=1, source_target_pairs={{8,0},{16,8},{24,16},{0,24},{9,1},{17,9},{25,17},{1,25},{10,2},{18... | collective-permute-start | bytes 786440 | tf_op jit(solution)/shard_map/ppermute | solution.py:115
  171.6 39.8 %collective-permute-start.11 = (bf16[512,256]{1,0:T(8,128)(2,1)S(1)}, bf16[512,256]{1,0:T(8,128)(2,1)S(1)}, u32[]{:S(2)}, u32[]{:S(2)}) collective-permute-start(bf16[512,256]{1,0:T(8,128)(2,1)S(1)} %copy-done), channel_id=1, source_target_pairs={{16,0},{24,8},{0,16},{8,24},{17,1},{25,9},{1,17},{9,25},{18,2},{26... | collective-permute-start | bytes 786440 | tf_op jit(solution)/shard_map/ppermute | solution.py:115
  184.2 27.8 %collective-permute-start.12 = (bf16[512,256]{1,0:T(8,128)(2,1)S(1)}, bf16[512,256]{1,0:T(8,128)(2,1)S(1)}, u32[]{:S(2)}, u32[]{:S(2)}) collective-permute-start(bf16[512,256]{1,0:T(8,128)(2,1)S(1)} %copy-done), channel_id=1, source_target_pairs={{24,0},{0,8},{8,16},{16,24},{25,1},{1,9},{9,17},{17,25},{26,2},{2,... | collective-permute-start | bytes 786440 | tf_op jit(solution)/shard_map/ppermute | solution.py:115
  222.1 20.1 %collective-permute-start.17 = (bf16[512,256]{1,0:T(8,128)(2,1)}, bf16[512,256]{1,0:T(8,128)(2,1)S(1)}, u32[]{:S(2)}, u32[]{:S(2)}) collective-permute-start(bf16[512,256]{1,0:T(8,128)(2,1)} %convert_element_type.21), channel_id=1, source_target_pairs={{5,0},{6,1},{7,2},{0,3},{1,4},{2,5},{3,6},{4,7},{13,8},{14,9},{15,... | collective-permute-start | bytes 786440 | tf_op jit(solution)/shard_map/ppermute | solution.py:115
  222.8 44.4 %collective-permute-start.16 = (bf16[512,256]{1,0:T(8,128)(2,1)}, bf16[512,256]{1,0:T(8,128)(2,1)S(1)}, u32[]{:S(2)}, u32[]{:S(2)}) collective-permute-start(bf16[512,256]{1,0:T(8,128)(2,1)} %convert_element_type.21), channel_id=1, source_target_pairs={{4,0},{5,1},{6,2},{7,3},{0,4},{1,5},{2,6},{3,7},{12,8},{13,9},{14,... | collective-permute-start | bytes 786440 | tf_op jit(solution)/shard_map/ppermute | solution.py:115
  226.5 41.8 %collective-permute-start.15 = (bf16[512,256]{1,0:T(8,128)(2,1)}, bf16[512,256]{1,0:T(8,128)(2,1)S(1)}, u32[]{:S(2)}, u32[]{:S(2)}) collective-permute-start(bf16[512,256]{1,0:T(8,128)(2,1)} %convert_element_type.21), channel_id=1, source_target_pairs={{3,0},{4,1},{5,2},{6,3},{7,4},{0,5},{1,6},{2,7},{11,8},{12,9},{13,... | collective-permute-start | bytes 786440 | tf_op jit(solution)/shard_map/ppermute | solution.py:115
  228.0 61.2 %collective-permute-start.14 = (bf16[512,256]{1,0:T(8,128)(2,1)}, bf16[512,256]{1,0:T(8,128)(2,1)S(1)}, u32[]{:S(2)}, u32[]{:S(2)}) collective-permute-start(bf16[512,256]{1,0:T(8,128)(2,1)} %convert_element_type.21), channel_id=1, source_target_pairs={{2,0},{3,1},{4,2},{5,3},{6,4},{7,5},{0,6},{1,7},{10,8},{11,9},{12,... | collective-permute-start | bytes 786440 | tf_op jit(solution)/shard_map/ppermute | solution.py:115
  230.4 59.9 %collective-permute-start.13 = (bf16[512,256]{1,0:T(8,128)(2,1)}, bf16[512,256]{1,0:T(8,128)(2,1)S(1)}, u32[]{:S(2)}, u32[]{:S(2)}) collective-permute-start(bf16[512,256]{1,0:T(8,128)(2,1)} %convert_element_type.21), channel_id=1, source_target_pairs={{1,0},{2,1},{3,2},{4,3},{5,4},{6,5},{7,6},{0,7},{9,8},{10,9},{11,1... | collective-permute-start | bytes 786440 | tf_op jit(solution)/shard_map/ppermute | solution.py:115
  242.1 50.9 %collective-permute-start.18 = (bf16[512,256]{1,0:T(8,128)(2,1)}, bf16[512,256]{1,0:T(8,128)(2,1)}, u32[]{:S(2)}, u32[]{:S(2)}) collective-permute-start(bf16[512,256]{1,0:T(8,128)(2,1)} %convert_element_type.21), channel_id=1, source_target_pairs={{6,0},{7,1},{0,2},{1,3},{2,4},{3,5},{4,6},{5,7},{14,8},{15,9},{8,1... | collective-permute-start | bytes 786440 | tf_op jit(solution)/shard_map/ppermute | solution.py:115
  267.2 28.6 %collective-permute-start.19 = (bf16[512,256]{1,0:T(8,128)(2,1)}, bf16[512,256]{1,0:T(8,128)(2,1)S(1)}, u32[]{:S(2)}, u32[]{:S(2)}) collective-permute-start(bf16[512,256]{1,0:T(8,128)(2,1)} %convert_element_type.21), channel_id=1, source_target_pairs={{7,0},{0,1},{1,2},{2,3},{3,4},{4,5},{5,6},{6,7},{15,8},{8,9},{9,10... | collective-permute-start | bytes 786440 | tf_op jit(solution)/shard_map/ppermute | solution.py:115
  292.6 4.6 %collective-permute-start.9 = (bf16[256,512]{1,0:T(8,128)(2,1)S(1)}, bf16[256,512]{1,0:T(8,128)(2,1)S(1)}, u32[]{:S(2)}, u32[]{:S(2)}) collective-permute-start(bf16[256,512]{1,0:T(8,128)(2,1)S(1)} %convert_element_type.19), channel_id=1, source_target_pairs={{24,0},{0,8},{8,16},{16,24},{25,1},{1,9},{9,17},{17,25},{26,2},{2,... | collective-permute-start | bytes 786440 | tf_op jit(solution)/shard_map/ppermute | solution.py:115
  294.2 10.4 %collective-permute-start.8 = (bf16[256,512]{1,0:T(8,128)(2,1)S(1)}, bf16[256,512]{1,0:T(8,128)(2,1)S(1)}, u32[]{:S(2)}, u32[]{:S(2)}) collective-permute-start(bf16[256,512]{1,0:T(8,128)(2,1)S(1)} %convert_element_type.19), channel_id=1, source_target_pairs={{16,0},{24,8},{0,16},{8,24},{17,1},{25,9},{1,17},{9,25},{18,2},{26... | collective-permute-start | bytes 786440 | tf_op jit(solution)/shard_map/ppermute | solution.py:115
  296.9 9.8 %collective-permute-start.7 = (bf16[256,512]{1,0:T(8,128)(2,1)S(1)}, bf16[256,512]{1,0:T(8,128)(2,1)S(1)}, u32[]{:S(2)}, u32[]{:S(2)}) collective-permute-start(bf16[256,512]{1,0:T(8,128)(2,1)S(1)} %convert_element_type.19), channel_id=1, source_target_pairs={{8,0},{16,8},{24,16},{0,24},{9,1},{17,9},{25,17},{1,25},{10,2},{18... | collective-permute-start | bytes 786440 | tf_op jit(solution)/shard_map/ppermute | solution.py:115
Sparse Core Ops, SparseCore 0:
  79.5 31.6 reduce-scatter.4
  125.6 154.4 reduce-scatter.2
